TPU v7x, 256 devices: a whole 4x4x8 slice. The times are simulated.
256 devices in a mesh: af: 4 (over z_hi), xr: 4 (over x), xc: 16 (over y, z_lo, core).
Axes of the slice: x: 4, y: 4, z: 8 (z_hi: 4, z_lo: 2; z = z_hi * 2 + z_lo), core: 2. Of those that a mesh axis runs over, the one named last changes fastest.
Arguments:
- samples: int32 [4096, 77824], P(('xr', 'xc', 'af')), may hold values from -8 to 7
- kept_channels: int32 [32], replicated, may hold values from 1 to 2047
- flags: int32 [4096], P(('xr', 'xc', 'af')), may hold values 0 or 1
Outputs:
- visibilities: bfloat16 [32, 2, 4096, 4096], P('af', None, 'xr', 'xc')
All inputs are finite; a program needn't handle non-finite values. No bound on the sum of `flags` on one device may be relied on, other than what follows from the above.
Results may differ from a plain program's by a relative error of at most 0.001.
Values sent between devices are 32-bit elements; how exact they have to be, the bound alone decides.
A program may use at most 64 MiB of HBM per device.

v0:
```python
import jax
import jax.numpy as jnp
from jax import lax
from jax.sharding import PartitionSpec as P

NFFT = 4096
TAPS = 4
SPEC = 16


def window_table(kept_channels, nfft, taps):
    length = taps * nfft
    points = jnp.arange(length, dtype=jnp.float32)
    window = jnp.sinc((points - length / 2 + 0.5) / nfft) * (
        0.5 - 0.5 * jnp.cos(2.0 * jnp.pi * (points + 0.5) / length)
    )
    window = window * (0.25 / jnp.sqrt(jnp.sum(window * window)))
    offsets = jnp.arange(nfft, dtype=jnp.int32)
    phases = kept_channels[:, None] * offsets[None, :] % nfft
    radians = 2.0 * jnp.pi / nfft * phases.astype(jnp.float32)
    shaped = window.reshape(taps, nfft)
    cosine = shaped[:, None, :] * jnp.cos(radians)[None]
    sine = -shaped[:, None, :] * jnp.sin(radians)[None]
    return jnp.stack([cosine, sine], axis=1)


def channelize(samples, flags, filter_table, spec_count):
    taps = filter_table.shape[0]
    nfft = filter_table.shape[3]
    inputs = samples.shape[0]
    blocks = samples.astype(jnp.float32).reshape(inputs, spec_count + taps - 1, nfft)
    summed = jnp.zeros((filter_table.shape[2], inputs, 2, spec_count), jnp.float32)
    for tap_index in range(taps):
        frames = blocks[:, tap_index : tap_index + spec_count, :]
        summed = summed + jnp.einsum(
            "pcn,isn->cips", filter_table[tap_index], frames, precision=lax.Precision.HIGHEST
        )
    summed = summed * flags.astype(jnp.float32)[None, :, None, None]
    return summed.reshape(summed.shape[0], inputs * 2 * spec_count)


def correlate(row_block, col_block, spec_count):
    real_part = col_block[..., :spec_count]
    imag_part = col_block[..., spec_count:]
    paired = jnp.concatenate([col_block, jnp.concatenate([-imag_part, real_part], axis=-1)], axis=1)
    product = jnp.einsum("cis,cjs->cij", row_block, paired, precision=lax.Precision.HIGHEST) * (
        1.0 / spec_count
    )
    col_count = col_block.shape[1]
    return jnp.stack([product[..., :col_count], product[..., col_count:]], axis=1).astype(
        jnp.bfloat16
    )


def shards(samples, kept_channels, flags):
    filter_table = window_table(kept_channels, NFFT, TAPS)
    spectra = channelize(samples, flags, filter_table, SPEC)
    turned = lax.all_to_all(spectra, "af", split_axis=0, concat_axis=1, tiled=True)
    channel_count = turned.shape[0]
    row_width = 2 * SPEC
    gridded = lax.all_gather(turned, ("xr", "xc"), axis=1, tiled=True)
    shaped = gridded.reshape(
        channel_count, lax.axis_size("xr"), lax.axis_size("xc"), turned.shape[1]
    )
    row_block = lax.dynamic_index_in_dim(shaped, lax.axis_index("xr"), 1, keepdims=False)
    col_block = lax.dynamic_index_in_dim(shaped, lax.axis_index("xc"), 2, keepdims=False)
    row_block = row_block.reshape(channel_count, -1, row_width)
    col_block = col_block.reshape(channel_count, -1, row_width)
    return correlate(row_block, col_block, SPEC)


def solution(mesh):
    return jax.shard_map(
        shards,
        mesh=mesh,
        in_specs=(P(("xr", "xc", "af"), None), P(), P(("xr", "xc", "af"))),
        out_specs=P("af", None, "xr", "xc"),
        check_vma=False,
    )
```

profile of v0, /device:TPU:1, one launch (start us, length us, event | category | flops | bytes accessed | tf_op | source)
XLA Modules:
  0.0 212.4 jit_solution(4326377731821453080)
XLA Ops:
  6.5 0.0 all-gather.2.cloned.1.call-start
  6.5 0.9 fusion.76
  8.2 0.6 fusion.77
  8.8 0.6 fusion.49
  9.5 2.8 %fusion.33 = (f32[32,4096]{1,0:T(8,128)S(1)}, f32[32,4096]{1,0:T(8,128)S(1)}) fusion(s32[32]{0:T(128)} %param.4), kind=kLoop, calls=%fused_computation.50 | loop fusion | flops 1835008 | bytes 1048704 | tf_op jit(solution)/shard_map/cos | solution.py:22
  12.2 5.0 %convert_element_type.23 = f32[16,77824]{1,0:T(8,128)} convert(s32[16,77824]{1,0:T(8,128)} %param.3) | non-fusion elementwise | flops 1245184 | bytes 9961472 | tf_op jit(solution)/shard_map/convert_element_type | solution.py:31
  17.2 5.0 %reshape.132 = f32[16,19,4096]{2,1,0:T(8,128)} reshape(f32[16,77824]{1,0:T(8,128)} %convert_element_type.23) | data formatting | bytes 9961472 | tf_op jit(solution)/shard_map/reshape | solution.py:31
  22.1 0.0 slice-start
  22.1 0.5 broadcast_multiply_fusion
  22.7 0.0 slice-start.1
  22.7 7.6 %fusion = f32[2,32,16,16]{1,3,2,0:T(8,128)S(1)} fusion(f32[16,19,4096]{2,1,0:T(8,128)} %reshape.132, f32[4,1,32,4096]{3,2,1,0:T(8,128)S(1)} %get-tuple-element.11, f32[4,1,32,4096]{3,2,1,0:T(8,128)S(1)} %get-tuple-element.12), kind=kOutput, calls=%fused_computation.11 | convolution fusion | flops 805568512 | bytes 8454144 | tf_op jit(solution)/shard_map/pcn,isn->cips/dot_general | solution.py:35
  30.3 0.0 slice-done
  30.4 0.0 slice-done.1
  30.4 3.4 %fusion.1 = f32[2,32,16,16]{1,3,2,0:T(8,128)S(1)} fusion(f32[16,19,4096]{2,1,0:T(8,128)S(1)} %bitcast.62, f32[4,1,32,4096]{3,2,1,0:T(8,128)S(1)} %get-tuple-element.12, f32[4,1,32,4096]{3,2,1,0:T(8,128)S(1)} %get-tuple-element.11), kind=kOutput, calls=%fused_computation.13 | convolution fusion | flops 805568512 | bytes 8454144 | tf_op jit(solution)/shard_map/pcn,isn->cips/dot_general | solution.py:35
  33.8 0.0 copy-start
  33.8 3.4 %fusion.2 = f32[2,32,16,16]{1,3,2,0:T(8,128)S(1)} fusion(f32[16,19,4096]{2,1,0:T(8,128)S(1)} %bitcast.62, f32[4,1,32,4096]{3,2,1,0:T(8,128)S(1)} %get-tuple-element.12, f32[4,1,32,4096]{3,2,1,0:T(8,128)S(1)} %get-tuple-element.11), kind=kOutput, calls=%fused_computation.15 | convolution fusion | flops 805568512 | bytes 8454144 | tf_op jit(solution)/shard_map/pcn,isn->cips/dot_general | solution.py:35
  37.3 0.0 copy-done
  37.3 3.5 %fusion.8 = f32[32,16,2,16]{0,3,1,2:T(8,128)S(1)} fusion(f32[2,32,16,16]{1,3,2,0:T(8,128)S(1)} %fusion, f32[2,32,16,16]{1,3,2,0:T(8,128)S(1)} %fusion.1, f32[2,32,16,16]{1,3,2,0:T(8,128)S(1)} %fusion.2, f32[16,19,4096]{2,1,0:T(8,128)S(1)} %bitcast.62, f32[4,1,32,4096]{3,2,1,0:T(8,128)S(1)} %get-tuple-element.12, ...), kind=kOutput, calls=%fused_computation.22 | convolution fusion | flops 805634048 | bytes 9241088 | tf_op jit(solution)/shard_map/pcn,isn->cips/dot_general | solution.py:35
  40.7 0.7 copy.12
  41.5 0.8 all_to_all.14
  42.2 16.0 %all_to_all.19 = f32[4,8,512]{2,1,0:T(8,128)} all-to-all(f32[4,8,512]{2,1,0:T(8,128)S(1)} %all_to_all.14), channel_id=1, replica_groups=mesh['af'=4,'xr'=4,'xc'=16] {'af'}, dimensions={0} | all-to-all | bytes 131072 | tf_op jit(solution)/shard_map/all_to_all | solution.py:58
  58.2 0.0 all-gather.2.cloned.1.call-update
  58.2 107.2 %all-gather.2.cloned.1.call-done = f32[8,131072]{1,0:T(8,128)} async-done(((f32[8,2048]{1,0:T(8,128)}), f32[8,131072]{1,0:T(8,128)}) %all-gather.2.cloned.1.call-update) | async-done | bytes 4194320 | tf_op jit(solution)/shard_map/all_gather | solution.py:61
  165.5 4.6 %copy.23 = f32[1,8,64,2048]{3,2,1,0:T(8,128)S(1)} copy(f32[1,8,64,2048]{3,1,2,0:T(8,128)} %bitcast.65) | data formatting | bytes 8388608
  170.1 0.7 dynamic-slice_reduce_fusion
  170.8 0.1 constant_dynamic-slice_fusion
  170.9 0.3 reshape.135
  171.3 0.3 copy.15
  171.6 2.7 %reshape.134 = f32[8,1024,32]{2,1,0:T(8,128)} reshape(f32[8,1,16,2048]{3,2,1,0:T(8,128)S(1)} %constant_dynamic-slice_fusion) | data formatting | bytes 2097152 | tf_op jit(solution)/shard_map/reshape | solution.py:67
  174.4 15.2 %multiply_convert_fusion = bf16[8,1024,512]{2,1,0:T(8,128)(2,1)S(1)} fusion(f32[8,1024,32]{2,1,0:T(8,128)} %reshape.134, f32[8,256,16]{1,2,0:T(8,128)S(1)} %get-tuple-element.8, f32[8,256,16]{1,2,0:T(8,128)S(1)} %get-tuple-element.7, f32[8,256,32]{1,2,0:T(8,128)S(1)} %copy.15), kind=kOutput, calls=%fused_computation | convolution fusion | flops 1619263488 | bytes 9961472 | tf_op jit(solution)/shard_map/cis,cjs->cij/dot_general | solution.py:46
  189.5 2.3 %slice_bitcast_fusion.1 = (bf16[8,1,1024,256]{3,2,0,1:T(8,128)(2,1)S(1)}, bf16[8,1,1024,256]{3,2,0,1:T(8,128)(2,1)}) fusion(bf16[8,1024,512]{2,1,0:T(8,128)(2,1)S(1)} %multiply_convert_fusion), kind=kLoop, calls=%fused_computation.9 | loop fusion | bytes 16777216 | tf_op jit(solution)/shard_map/stack | solution.py:50
  191.8 6.2 %pad_maximum_fusion = bf16[8,2,1024,256]{3,2,0,1:T(8,128)(2,1)} fusion(bf16[8,1,1024,256]{3,2,0,1:T(8,128)(2,1)} %get-tuple-element.6, bf16[8,1,1024,256]{3,2,0,1:T(8,128)(2,1)S(1)} %get-tuple-element.5), kind=kLoop, calls=%fused_computation.1 | loop fusion | flops 4194304 | bytes 16777216 | tf_op jit(solution)/shard_map/stack | solution.py:50
  198.0 7.5 %copy.17 = bf16[8,2,1024,256]{3,2,1,0:T(8,128)(2,1)} copy(bf16[8,2,1024,256]{3,2,0,1:T(8,128)(2,1)} %pad_maximum_fusion) | data formatting | bytes 16777216 | tf_op jit(solution)/shard_map/stack | solution.py:50
  (3 shorter events, 0.0 us)
Async XLA Ops:
  6.5 158.9 %all-gather.2.cloned.1.call-start = ((), (), s32[]{:S(2)}) async-start(), calls=%async_computation.1 | async-start | bytes 4259840 | tf_op jit(solution)/shard_map/all_gather | solution.py:61
  22.1 8.2 %slice-start = ((s8[6291456]{0:T(1024)(128)(4,1)}), s8[2097152]{0:T(1024)(128)(4,1)S(1)}, s32[]{:S(2)}) async-start(s8[6291456]{0:T(1024)(128)(4,1)} %bitcast.61), calls=%async_computation.2 | async-start | bytes 4194304
  22.7 7.7 %slice-start.1 = ((s8[6291456]{0:T(1024)(128)(4,1)}), s8[4194304]{0:T(1024)(128)(4,1)S(1)}, s32[]{:S(2)}) async-start(s8[6291456]{0:T(1024)(128)(4,1)} %bitcast.61), calls=%async_computation.3 | async-start | bytes 8388608
  33.8 3.4 %copy-start = (s32[16]{0:T(128)S(1)}, s32[16]{0:T(128)}, u32[]{:S(2)}) copy-start(s32[16]{0:T(128)} %param.5) | copy-start | bytes 196
Sparse Core Ops, SparseCore 0:
  58.3 107.0 all-gather.1
where the time goes:
time: 213 us; the launch traced here: 212 us
  waiting for transfers between devices  107 us (50%)
  matrix products  33.1 us (16%)
  local copies, waits for them, and re-layouts  25.1 us (12%)
  other arithmetic  16.7 us (8%)
  blocking collectives  16 us (8%)
  between operations  14.2 us (7%)
    all_gather x1, waiting for transfers between devices, shards(): gridded = lax.all_gather(turned, ('xr', 'xc'), axis=1, tiled=True)  107 us
    dot_general x4, matrix products, channelize(): jnp.einsum('pcn,isn->cips', filter_table[tap_index], frames, precision=la...  17.9 us
    all_to_all x1, blocking collectives, shards(): lax.all_to_all(spectra, 'af', split_axis=0, concat_axis=1, tiled=True)  16 us
    dot_general x1, matrix products, correlate(): jnp.einsum('cis,cjs->cij', row_block, paired, precision=lax.Precision.HIG...  15.2 us
    another operation x2, local copies, waits for them, and re-layouts, correlate(): jnp.stack([product[..., :col_count], product[..., col_count:]], axis=1)  9.82 us
    another operation x1, other arithmetic, correlate(): jnp.stack([product[..., :col_count], product[..., col_count:]], axis=1)  6.18 us
    reshape x1, local copies, waits for them, and re-layouts, channelize(): samples.astype(jnp.float32).reshape(inputs, spec_count + taps - 1, nfft)  4.97 us
    convert_element_type x1, other arithmetic, channelize(): samples.astype(jnp.float32).reshape(inputs, spec_count + taps - 1, nfft)  4.96 us
  transfers between devices with their start and end apart: 1, of which 1 were waited for; matrix products, arithmetic and copies ran while one was open for 0% of the time, Pallas kernels for 0%

commit v1 on v0

v1 whole, which is shorter than its diff:
```python
import functools
import math

import jax
import jax.numpy as jnp
from jax import lax
from jax.experimental import pallas as pl
from jax.experimental.pallas import tpu as pltpu
from jax.sharding import PartitionSpec as P

NFFT = 4096
TAPS = 4
SPEC = 16
BLOCKS = SPEC + TAPS - 1
CHUNKS = 4
CHUNK = NFFT // CHUNKS
MESH = pl.DeviceIdType.MESH
NT = (((1,), (1,)), ((), ()))


def sincos(phase, period):
    quarter = period // 4
    turned = phase + quarter // 2
    rest = (turned & (quarter - 1)) - quarter // 2
    quadrant = lax.shift_right_logical(turned, int(math.log2(quarter))) & 3
    angle = rest.astype(jnp.float32) * (2.0 * math.pi / period)
    z = angle * angle
    s = angle * (1.0 + z * (-1.0 / 6 + z * (1.0 / 120 + z * (-1.0 / 5040 + z * (1.0 / 362880)))))
    c = 1.0 + z * (-0.5 + z * (1.0 / 24 + z * (-1.0 / 720 + z * (1.0 / 40320))))
    odd = (quadrant & 1) == 1
    sine = jnp.where(odd, c, s)
    cosine = jnp.where(odd, s, c)
    sine = jnp.where(quadrant >= 2, -sine, sine)
    cosine = jnp.where((quadrant == 1) | (quadrant == 2), -cosine, cosine)
    return sine, cosine


def spread(
    samples, kept, flags, rows, cols, raw, frames, table, window, blocks,
    load_sem, turn_send, turn_recv, row_send, row_recv, col_send, col_recv,
):
    f, r, k = lax.axis_index("af"), lax.axis_index("xr"), lax.axis_index("xc")
    y, zl, core = k // 4, (k // 2) % 2, k % 2

    for part in range(CHUNKS):
        for b in range(BLOCKS):
            pltpu.make_async_copy(
                samples.at[:, pl.ds(b * NFFT + part * CHUNK, CHUNK)], raw.at[part, b], load_sem.at[part]
            ).start()

    def slot(yy, zz, cc):
        return (yy * 2 + zz) * 2 + cc

    y_peers = [slot((y + d) % 4, zl, core) for d in (1, 3, 2)]
    z_peer = slot(y, 1 - zl, core)
    c_peer = slot(y, zl, 1 - core)
    x_peers = [(r + d) % 4 for d in (1, 3, 2)]
    f_peers = [(f + d) % 4 for d in (1, 3, 2)]

    barrier = pltpu.get_barrier_semaphore()
    for peer in f_peers:
        pl.semaphore_signal(barrier, inc=1, device_id={"af": peer}, device_id_type=MESH)
    for peer in x_peers:
        pl.semaphore_signal(barrier, inc=1, device_id={"xr": peer}, device_id_type=MESH)
    for peer in y_peers + [z_peer, c_peer]:
        pl.semaphore_signal(barrier, inc=1, device_id={"xc": peer}, device_id_type=MESH)

    lane = lax.broadcasted_iota(jnp.int32, (64, 128), 1)
    line = lax.broadcasted_iota(jnp.int32, (64, 128), 0)
    channel = ((line >> 2) & 7) * 4 + (line >> 5) * 2 + ((line >> 1) & 1)
    kept_line = jnp.zeros((64, 128), jnp.int32)
    for j in range(32):
        kept_line = jnp.where(channel == j, kept[j], kept_line)
    quarter_turn = (line & 1) * (NFFT // 4)
    coarse_s, coarse_c = sincos((kept_line * (128 * (lane & 31)) + quarter_turn) & (NFFT - 1), NFFT)
    fine_s, fine_c = sincos((kept_line * lane) & (NFFT - 1), NFFT)

    odd = (
        2 * (lax.broadcasted_iota(jnp.int32, (128, 128), 0) * 128 + lax.broadcasted_iota(jnp.int32, (128, 128), 1))
        - (TAPS * NFFT - 1)
    )
    ws, wc = sincos(odd & (8 * NFFT - 1), 8 * NFFT)
    shape = ws * wc / (odd.astype(jnp.float32) * (2.0 * math.pi / (8 * NFFT))) * (0.5 + 0.5 * wc)
    window[...] = shape
    total = jnp.sum(jnp.sum(shape * shape, axis=0, keepdims=True), axis=1, keepdims=True)
    scale = 0.25 * lax.rsqrt(total)

    summed = None
    for part in range(CHUNKS):
        for a in range(part * CHUNK // 128, (part + 1) * CHUNK // 128):
            trig = coarse_c[:, a : a + 1] * fine_c - coarse_s[:, a : a + 1] * fine_s
            for t in range(TAPS):
                value = trig * window[t * 32 + a : t * 32 + a + 1, :]
                high = value.astype(jnp.bfloat16)
                low = (value - high.astype(jnp.float32)).astype(jnp.bfloat16)
                for half in range(2):
                    at = (t // 2) * 128 + half * 64 + (t % 2) * 32
                    table[at : at + 32, a * 128 : (a + 1) * 128] = high[half * 32 : half * 32 + 32]
                    table[256 + at : 256 + at + 32, a * 128 : (a + 1) * 128] = low[half * 32 : half * 32 + 32]
        pltpu.make_async_copy(raw.at[part], raw.at[part], load_sem.at[part]).wait()
        span = slice(part * CHUNK, (part + 1) * CHUNK)
        for b in range(BLOCKS):
            frames[b * 16 : (b + 1) * 16, span] = raw[part, b].astype(jnp.float32).astype(jnp.bfloat16)
        product = lax.dot_general(frames[:, span], table[:, span], NT, preferred_element_type=jnp.float32)
        summed = product if summed is None else summed + product

    summed = summed[:, :256] + summed[:, 256:]
    first, second = summed[:, :128], summed[:, 128:]
    wide_lane = lax.broadcasted_iota(jnp.int32, (256, 128), 1)
    tapped = jnp.where(
        (wide_lane & 32) == 0, first[0:256] + second[32:288], first[16:272] + second[48:304]
    )
    lane = lax.broadcasted_iota(jnp.int32, (128, 128), 1)
    low_tap = (lane & 32) == 0
    early, late = tapped[:128], tapped[128:]
    crossed = jnp.where(low_tap, late, early)
    crossed = jnp.where(low_tap, pltpu.roll(crossed, 96, 1), pltpu.roll(crossed, 32, 1))
    both = jnp.where(low_tap, early, late) + crossed
    tiles = [both[16 * j : 16 * j + 16] for j in range(8)]
    lane = lax.broadcasted_iota(jnp.int32, (16, 128), 1)
    for bit in range(3):
        step = 4 << bit
        low_lane = (lane & step) == 0
        for j in range(8):
            if j & (1 << bit):
                continue
            zero, one = tiles[j], tiles[j | (1 << bit)]
            tiles[j] = jnp.where(low_lane, zero, pltpu.roll(one, step, 1))
            tiles[j | (1 << bit)] = jnp.where(low_lane, pltpu.roll(zero, 128 - step, 1), one)
    row = lax.broadcasted_iota(jnp.int32, (16, 128), 0)
    gain = jnp.zeros((16, 128), jnp.int32)
    for j in range(16):
        gain = jnp.where(row == j, flags[j], gain)
    gain = gain.astype(jnp.float32) * scale
    for j in range(8):
        blocks[j // 2, j % 2] = tiles[j] * gain

    pl.semaphore_wait(barrier, 11)

    def turn(d, peer):
        return pltpu.make_async_remote_copy(
            src_ref=blocks.at[peer],
            dst_ref=rows.at[k, :, pl.ds(pl.multiple_of(f * 16, 16), 16), :],
            send_sem=turn_send.at[d],
            recv_sem=turn_recv.at[d],
            device_id={"af": peer},
            device_id_type=MESH,
        )

    turns = [turn(d, peer) for d, peer in enumerate(f_peers)]
    for copy in turns:
        copy.start()
    rows[k, :, pl.ds(pl.multiple_of(f * 16, 16), 16), :] = blocks[f]
    for copy in turns:
        copy.wait()

    def spread_row(number, which, peer):
        return pltpu.make_async_remote_copy(
            src_ref=rows.at[which],
            dst_ref=rows.at[which],
            send_sem=row_send.at[number],
            recv_sem=row_recv.at[number],
            device_id={"xc": peer},
            device_id_type=MESH,
        )

    def spread_col(number, peer):
        return pltpu.make_async_remote_copy(
            src_ref=rows.at[k],
            dst_ref=cols.at[r],
            send_sem=col_send.at[number],
            recv_sem=col_recv.at[number],
            device_id={"xr": peer},
            device_id_type=MESH,
        )

    started = []

    def go(copy):
        copy.start()
        started.append(copy)
        return copy

    along_y = [go(spread_row(n, k, peer)) for n, peer in enumerate(y_peers)]
    along_z = [go(spread_row(3, k, z_peer))]
    between = [go(spread_row(7, k, c_peer))]
    along_x = [go(spread_col(n, peer)) for n, peer in enumerate(x_peers)]
    cols[r] = rows[k]
    sources = [slot((y - d) % 4, zl, core) for d in (1, 3, 2)]
    for n, source in enumerate(sources):
        along_y[n].wait_recv()
        along_z.append(go(spread_row(4 + n, source, z_peer)))
        between.append(go(spread_row(8 + n, source, c_peer)))
    partners = [slot(y, 1 - zl, core)] + [slot((y - d) % 4, 1 - zl, core) for d in (1, 3, 2)]
    for n, source in enumerate(partners):
        along_z[n].wait_recv()
        between.append(go(spread_row(11 + n, source, c_peer)))
    for copy in between + along_x:
        copy.wait_recv()
    for copy in started:
        copy.wait_send()


def correlate(rows, cols, out, left, stage, out_sem):
    lane = lax.broadcasted_iota(jnp.int32, (256, 128), 1)
    real_lane = (lane & 1) == 0

    def step(number, _):
        c_hi, p = number // 2, number % 2
        long_lane = lax.broadcasted_iota(jnp.int32, (1024, 128), 1)
        x = rows[:, c_hi].reshape(1024, 128)
        high = x.astype(jnp.bfloat16)
        low = (x - high.astype(jnp.float32)).astype(jnp.bfloat16)
        left[:, :128] = jnp.where((long_lane >> 6) == p, x, pltpu.roll(x, 64, 1)).astype(jnp.bfloat16)
        left[:, 128:] = low
        operand = left[...]
        mine = (lane >> 6) == p
        c = cols[:, c_hi].reshape(256, 128) * (1.0 / SPEC)
        c = jnp.where(mine, c, pltpu.roll(c, 64, 1))
        swapped = jnp.where(real_lane, -pltpu.roll(c, 127, 1), pltpu.roll(c, 1, 1))
        for part, value in enumerate((c, swapped)):
            value_high = value.astype(jnp.bfloat16).astype(jnp.float32)
            value_low = value - value_high
            first = jnp.where(lane < 64, value_high, value_low)
            for e in range(2):
                mask = ((lane >> 1) & 1) == e
                right = jnp.concatenate(
                    [jnp.where(mask, first, 0.0), jnp.where(mask & mine, value_high, 0.0)], axis=1
                ).astype(jnp.bfloat16)
                product = lax.dot_general(operand, right, NT, preferred_element_type=jnp.float32)
                channel = number * 2 + e
                stage[channel, part] = product.astype(jnp.bfloat16)
                pltpu.make_async_copy(
                    stage.at[channel, part], out.at[channel, part], out_sem.at[channel, part]
                ).start()
        return 0

    lax.fori_loop(0, 4, step, 0)

    def finish(channel, _):
        for part in range(2):
            pltpu.make_async_copy(
                stage.at[channel, part], out.at[channel, part], out_sem.at[channel, part]
            ).wait()
        return 0

    lax.fori_loop(0, 8, finish, 0)


def shards(samples, kept_channels, flags):
    vmem = pl.BlockSpec(memory_space=pltpu.VMEM)
    smem = pl.BlockSpec(memory_space=pltpu.SMEM)
    hbm = pl.BlockSpec(memory_space=pl.ANY)
    dma = pltpu.SemaphoreType.DMA
    rows, cols = pl.pallas_call(
        spread,
        out_shape=[pltpu.VMEM((16, 2, 64, 128), jnp.float32), pltpu.VMEM((4, 2, 64, 128), jnp.float32)],
        in_specs=[hbm, smem, smem],
        out_specs=[vmem, vmem],
        scratch_shapes=[
            pltpu.VMEM((CHUNKS, BLOCKS, 16, CHUNK), jnp.int32),
            pltpu.VMEM((BLOCKS * 16, NFFT), jnp.bfloat16),
            pltpu.VMEM((512, NFFT), jnp.bfloat16),
            pltpu.VMEM((128, 128), jnp.float32),
            pltpu.VMEM((4, 2, 16, 128), jnp.float32),
            dma((CHUNKS,)),
            dma((3,)),
            dma((3,)),
            dma((15,)),
            dma((15,)),
            dma((3,)),
            dma((3,)),
        ],
        compiler_params=pltpu.CompilerParams(
            collective_id=0, has_side_effects=True, vmem_limit_bytes=40 * 1024 * 1024
        ),
        name="spread",
    )(samples, kept_channels, flags)
    return pl.pallas_call(
        correlate,
        out_shape=jax.ShapeDtypeStruct((8, 2, 1024, 256), jnp.bfloat16),
        in_specs=[vmem, vmem],
        out_specs=hbm,
        scratch_shapes=[
            pltpu.VMEM((1024, 256), jnp.bfloat16),
            pltpu.VMEM((8, 2, 1024, 256), jnp.bfloat16),
            dma((8, 2)),
        ],
        compiler_params=pltpu.CompilerParams(vmem_limit_bytes=40 * 1024 * 1024),
        name="correlate",
    )(rows, cols)


def solution(mesh):
    return jax.shard_map(
        shards,
        mesh=mesh,
        in_specs=(P(("xr", "xc", "af"), None), P(), P(("xr", "xc", "af"))),
        out_specs=P("af", None, "xr", "xc"),
        check_vma=False,
    )
```

time: 213 us -> 39.3 us (0.18)
  waiting for transfers between devices: 107 us -> 0 us
  Pallas kernels: 0 us -> 35.5 us
  matrix products: 33.1 us -> 0 us
  local copies, waits for them, and re-layouts: 25.1 us -> 3.72 us
  other arithmetic: 16.7 us -> 0 us
  blocking collectives: 16 us -> 0 us
  between operations: 14.2 us -> 0.01 us
    all_gather x1 -> x0, waiting for transfers between devices: 107 us -> none  [shards(): gridded = lax.all_gather(turned, ('xr', 'xc'), axis=1, tiled=True)]
    pallas_call x0 -> x2, Pallas kernels: none -> 35.5 us  [the longest x1 30.5 us: shards(): pl.pallas_call(spread, out_shape=[pltpu.VMEM((16, 2, 64, 128), jnp.float3...]
    dot_general x5 -> x0, matrix products: 33.1 us -> none  [the longest x4 17.9 us: channelize(): jnp.einsum('pcn,isn->cips', filter_table[tap_index], frames, precision=la...]
    all_to_all x1 -> x0, blocking collectives: 16 us -> none  [shards(): lax.all_to_all(spectra, 'af', split_axis=0, concat_axis=1, tiled=True)]
    another operation x2 -> x0, local copies, waits for them, and re-layouts: 9.82 us -> none  [correlate(): jnp.stack([product[..., :col_count], product[..., col_count:]], axis=1)]
    reshape x4 -> x0, local copies, waits for them, and re-layouts: 8.35 us -> none  [the longest x1 4.97 us: channelize(): samples.astype(jnp.float32).reshape(inputs, spec_count + taps - 1, nfft)]
    another operation x1 -> x0, other arithmetic: 6.18 us -> none  [correlate(): jnp.stack([product[..., :col_count], product[..., col_count:]], axis=1)]
    convert_element_type x2 -> x0, other arithmetic: 4.96 us -> none  [the longest x1 4.96 us: channelize(): samples.astype(jnp.float32).reshape(inputs, spec_count + taps - 1, nfft)]
  transfers between devices with their start and end apart: 1 -> 0, of which waited for: 1 -> 0; matrix products, arithmetic and copies ran while one was open for 0% -> 0% of each run, Pallas kernels for 0% -> 0%
where the time goes in v1:
time: 39.3 us; the launch traced here: 39.2 us
  Pallas kernels  35.5 us (90%)
  local copies, waits for them, and re-layouts  3.72 us (9%)
    pallas_call x1, Pallas kernels, shards(): pl.pallas_call(spread, out_shape=[pltpu.VMEM((16, 2, 64, 128), jnp.float3...  30.5 us
    pallas_call x1, Pallas kernels, shards(): pl.pallas_call(correlate, out_shape=jax.ShapeDtypeStruct((8, 2, 1024, 256...  4.92 us
    unnamed x6, local copies, waits for them, and re-layouts  3.72 us

profile of v1, /device:TPU:1, one launch (start us, length us, event | category | flops | bytes accessed | tf_op | source)
XLA Modules:
  0.0 39.2 jit_solution(14936486462266452102)
XLA Ops:
  0.0 0.0 copy-start
  0.0 2.4 %copy-done = s32[16,77824]{1,0:T(8,128)S(1)} copy-done((s32[16,77824]{1,0:T(8,128)S(1)}, s32[16,77824]{1,0:T(8,128)}, u32[]{:S(2)}) %copy-start) | copy-done | bytes 4980760
  2.4 0.0 copy-start.1
  2.4 0.7 %copy-done.1 = s32[32]{0:T(128)S(1)} copy-done((s32[32]{0:T(128)S(1)}, s32[32]{0:T(128)}, u32[]{:S(2)}) %copy-start.1) | copy-done | bytes 152
  3.1 0.0 copy-start.2
  3.1 0.7 %copy-done.2 = s32[16]{0:T(128)S(1)} copy-done((s32[16]{0:T(128)S(1)}, s32[16]{0:T(128)}, u32[]{:S(2)}) %copy-start.2) | copy-done | bytes 88
  3.7 30.5 %spread.1 = (f32[16,2,64,128]{3,2,1,0:T(8,128)S(1)}, f32[4,2,64,128]{3,2,1,0:T(8,128)S(1)}) custom-call(s32[16,77824]{1,0:T(8,128)S(1)} %copy-done, s32[32]{0:T(128)S(1)} %copy-done.1, s32[16]{0:T(128)S(1)} %copy-done.2), custom_call_target="tpu_custom_call" | custom-call | tf_op jit(solution)/shard_map/spread/pallas_call | solution.py:255
  34.3 4.9 %correlate.1 = bf16[8,2,1024,256]{3,2,1,0:T(8,128)(2,1)} custom-call(f32[16,2,64,128]{3,2,1,0:T(8,128)S(1)} %get-tuple-element.7.rows, f32[4,2,64,128]{3,2,1,0:T(8,128)S(1)} %get-tuple-element.8.cols), custom_call_target="tpu_custom_call" | custom-call | tf_op jit(solution)/shard_map/correlate/pallas_call | solution.py:279
Async XLA Ops:
  0.0 2.4 %copy-start = (s32[16,77824]{1,0:T(8,128)S(1)}, s32[16,77824]{1,0:T(8,128)}, u32[]{:S(2)}) copy-start(s32[16,77824]{1,0:T(8,128)} %samples.1) | copy-start | bytes 14942212
  2.4 0.7 %copy-start.1 = (s32[32]{0:T(128)S(1)}, s32[32]{0:T(128)}, u32[]{:S(2)}) copy-start(s32[32]{0:T(128)} %kept.1) | copy-start | bytes 388
  3.1 0.7 %copy-start.2 = (s32[16]{0:T(128)S(1)}, s32[16]{0:T(128)}, u32[]{:S(2)}) copy-start(s32[16]{0:T(128)} %flags.1) | copy-start | bytes 196

commit v2 on v1

v2 whole, which is shorter than its diff:
```python
import functools
import math

import jax
import jax.numpy as jnp
from jax import lax
from jax.experimental import pallas as pl
from jax.experimental.pallas import tpu as pltpu
from jax.sharding import PartitionSpec as P

NFFT = 4096
TAPS = 4
SPEC = 16
BLOCKS = SPEC + TAPS - 1
CHUNKS = 4
CHUNK = NFFT // CHUNKS
MESH = pl.DeviceIdType.MESH
NT = (((1,), (1,)), ((), ()))
UNITS = (
    ((0, 0), (1, 1), (7, 1), (1, 0), (7, 0), (6, 1), (6, 0), (2, 0)),
    ((0, 1), (2, 1), (3, 1), (5, 1), (3, 0), (5, 0), (4, 1), (4, 0)),
)
Z_ORDER = (4, 3, 5, 2, 6, 1, 7)
ARRIVALS = (
    ("z", 1), ("z", 2), ("y", 1, 0), ("y", 3, 0), ("z", 3), ("z", 4), ("y", 2, 0), ("z", 5), ("z", 6), ("z", 7),
    *(("y", dy, j) for j in range(1, 8) for dy in (1, 3, 2)),
)


def sincos(phase, period):
    quarter = period // 4
    turned = phase + quarter // 2
    rest = (turned & (quarter - 1)) - quarter // 2
    quadrant = lax.shift_right_logical(turned, int(math.log2(quarter))) & 3
    angle = rest.astype(jnp.float32) * (2.0 * math.pi / period)
    z = angle * angle
    s = angle * (1.0 + z * (-1.0 / 6 + z * (1.0 / 120 + z * (-1.0 / 5040 + z * (1.0 / 362880)))))
    c = 1.0 + z * (-0.5 + z * (1.0 / 24 + z * (-1.0 / 720 + z * (1.0 / 40320))))
    odd = (quadrant & 1) == 1
    sine = jnp.where(odd, c, s)
    cosine = jnp.where(odd, s, c)
    sine = jnp.where(quadrant >= 2, -sine, sine)
    cosine = jnp.where((quadrant == 1) | (quadrant == 2), -cosine, cosine)
    return sine, cosine


def spread(
    samples, kept_hbm, flags_hbm, rows, cols, raw, frames, table, window, blocks, kept, flags,
    load_sem, small_sem, z_send, z_recv, y_send, y_recv, c_send, c_recv, x_send, x_recv,
):
    f, r, k = lax.axis_index("af"), lax.axis_index("xr"), lax.axis_index("xc")
    y, zl, core = k // 4, (k // 2) % 2, k % 2
    z = f * 2 + zl

    small = [
        pltpu.make_async_copy(kept_hbm, kept, small_sem.at[0]),
        pltpu.make_async_copy(flags_hbm, flags, small_sem.at[1]),
    ]
    for copy in small:
        copy.start()
    for part in range(CHUNKS):
        for b in range(BLOCKS):
            pltpu.make_async_copy(
                samples.at[:, pl.ds(b * NFFT + part * CHUNK, CHUNK)], raw.at[part, b], load_sem.at[part]
            ).start()

    def pick(pair):
        return pair[0] if pair[0] == pair[1] else pair[0] + core * (pair[1] - pair[0])

    def on_z(d, cc):
        zz = (z + d) % 8
        return {"af": zz // 2, "xc": y * 4 + (zz % 2) * 2 + cc}

    y_peers = {d: {"xc": ((y + d) % 4) * 4 + zl * 2 + core} for d in (1, 3, 2)}
    c_peer = {"xc": k + 1 - 2 * core}

    def on_x(d, cc):
        return {"xr": (r + d) % 4, "xc": y * 4 + zl * 2 + cc}

    barrier = pltpu.get_barrier_semaphore()
    greeted = [on_z(d, cc) for d in range(1, 8) for cc in range(2)] + [on_x(d, cc) for d in range(1, 4) for cc in range(2)]
    greeted += [*y_peers.values(), c_peer]
    for peer in greeted:
        pl.semaphore_signal(barrier, inc=1, device_id=peer, device_id_type=MESH)

    odd = (
        2 * (lax.broadcasted_iota(jnp.int32, (128, 128), 0) * 128 + lax.broadcasted_iota(jnp.int32, (128, 128), 1))
        - (TAPS * NFFT - 1)
    )
    ws, wc = sincos(odd & (8 * NFFT - 1), 8 * NFFT)
    shape = ws * wc / (odd.astype(jnp.float32) * (2.0 * math.pi / (8 * NFFT))) * (0.5 + 0.5 * wc)
    window[...] = shape
    total = jnp.sum(jnp.sum(shape * shape, axis=0, keepdims=True), axis=1, keepdims=True)
    scale = 0.25 * lax.rsqrt(total)

    for copy in small:
        copy.wait()

    lane = lax.broadcasted_iota(jnp.int32, (64, 128), 1)
    line = lax.broadcasted_iota(jnp.int32, (64, 128), 0)
    channel = ((line >> 2) & 7) * 4 + (line >> 5) * 2 + ((line >> 1) & 1)
    kept_line = jnp.zeros((64, 128), jnp.int32)
    for j in range(32):
        kept_line = jnp.where(channel == j, kept[j], kept_line)
    quarter_turn = (line & 1) * (NFFT // 4)
    coarse_s, coarse_c = sincos((kept_line * (128 * (lane & 31)) + quarter_turn) & (NFFT - 1), NFFT)
    fine_s, fine_c = sincos((kept_line * lane) & (NFFT - 1), NFFT)

    summed = None
    for part in range(CHUNKS):
        for a in range(part * CHUNK // 128, (part + 1) * CHUNK // 128):
            trig = coarse_c[:, a : a + 1] * fine_c - coarse_s[:, a : a + 1] * fine_s
            for t in range(TAPS):
                value = trig * window[t * 32 + a : t * 32 + a + 1, :]
                high = value.astype(jnp.bfloat16)
                low = (value - high.astype(jnp.float32)).astype(jnp.bfloat16)
                for half in range(2):
                    at = (t // 2) * 128 + half * 64 + (t % 2) * 32
                    table[at : at + 32, a * 128 : (a + 1) * 128] = high[half * 32 : half * 32 + 32]
                    table[256 + at : 256 + at + 32, a * 128 : (a + 1) * 128] = low[half * 32 : half * 32 + 32]
        pltpu.make_async_copy(raw.at[part], raw.at[part], load_sem.at[part]).wait()
        span = slice(part * CHUNK, (part + 1) * CHUNK)
        for b in range(BLOCKS):
            frames[b * 16 : (b + 1) * 16, span] = raw[part, b].astype(jnp.float32).astype(jnp.bfloat16)
        product = lax.dot_general(frames[:, span], table[:, span], NT, preferred_element_type=jnp.float32)
        summed = product if summed is None else summed + product

    summed = summed[:, :256] + summed[:, 256:]
    first, second = summed[:, :128], summed[:, 128:]
    wide_lane = lax.broadcasted_iota(jnp.int32, (256, 128), 1)
    tapped = jnp.where(
        (wide_lane & 32) == 0, first[0:256] + second[32:288], first[16:272] + second[48:304]
    )
    lane = lax.broadcasted_iota(jnp.int32, (128, 128), 1)
    low_tap = (lane & 32) == 0
    early, late = tapped[:128], tapped[128:]
    crossed = jnp.where(low_tap, late, early)
    crossed = jnp.where(low_tap, pltpu.roll(crossed, 96, 1), pltpu.roll(crossed, 32, 1))
    both = jnp.where(low_tap, early, late) + crossed
    tiles = [both[16 * j : 16 * j + 16] for j in range(8)]
    lane = lax.broadcasted_iota(jnp.int32, (16, 128), 1)
    for bit in range(3):
        step = 4 << bit
        low_lane = (lane & step) == 0
        for j in range(8):
            if j & (1 << bit):
                continue
            zero, one = tiles[j], tiles[j | (1 << bit)]
            tiles[j] = jnp.where(low_lane, zero, pltpu.roll(one, step, 1))
            tiles[j | (1 << bit)] = jnp.where(low_lane, pltpu.roll(zero, 128 - step, 1), one)
    row = lax.broadcasted_iota(jnp.int32, (16, 128), 0)
    gain = jnp.zeros((16, 128), jnp.int32)
    for j in range(16):
        gain = jnp.where(row == j, flags[j], gain)
    gain = gain.astype(jnp.float32) * scale
    for j in range(8):
        blocks[j // 2, j % 2] = tiles[j] * gain

    pl.semaphore_wait(barrier, len(greeted))

    started = []

    def copy_to(src, dst, sems, send_at, recv_at, peer):
        return pltpu.make_async_remote_copy(
            src_ref=src,
            dst_ref=dst,
            send_sem=sems[0].at[send_at],
            recv_sem=sems[1].at[recv_at],
            device_id=peer,
            device_id_type=MESH,
        )

    def send(src, dst, sems, at, peer):
        copy = copy_to(src, dst, sems, at, at, peer)
        copy.start()
        started.append(copy)
        return copy

    def arrived(block, sem):
        pltpu.make_async_copy(block, block, sem).wait()

    def place(ref, dy, dz, cc):
        yy, zz = (y - dy) % 4, (z - dz) % 8
        return ref.at[yy, zz % 2, cc, zz // 2]

    def unit(j):
        return tuple(pick((UNITS[0][j][n], UNITS[1][j][n])) for n in range(2))

    along_y, across = {}, {}
    mine = place(rows, 0, 0, core)
    for d in Z_ORDER:
        hosts = [next((cc, j) for cc in range(2) for j in range(8) if UNITS[cc][j] == (d, source)) for source in range(2)]
        copy = copy_to(
            blocks.at[((z + d) % 8) // 2],
            mine,
            (z_send, z_recv),
            (d,),
            (pick((hosts[0][1], hosts[1][1])),),
            on_z(d, pick((hosts[0][0], hosts[1][0]))),
        )
        copy.start()
        started.append(copy)
    mine[...] = blocks[f]

    def to_columns(j, d, slot):
        dz, source = unit(j)
        return copy_to(
            place(rows, 0, dz, source),
            cols.at[r, ((z - dz) % 8) // 2],
            (x_send, x_recv),
            (d, slot),
            (d, dz // 2),
            on_x(d, source),
        )

    def forward(j):
        block = place(rows, 0, *unit(j))
        for d, peer in y_peers.items():
            along_y[d, j] = send(block, block, (y_send, y_recv), (d, j), peer)
        slots = [
            [i for i in range(8) if UNITS[cc][i][0] % 2 == 0].index(j) if UNITS[cc][j][0] % 2 == 0 else None
            for cc in range(2)
        ]
        for d in (1, 3, 2):
            if slots[0] == slots[1] and slots[0] is not None:
                to_columns(j, d, slots[0]).start()
            elif slots != [None, None]:
                owner = 0 if slots[1] is None else 1

                @pl.when(core == owner)
                def _():
                    to_columns(j, d, slots[owner]).start()

        share(0, j)

    def share(dy, j):
        block = place(rows, dy, *unit(j))
        across[dy, j] = send(block, block, (c_send, c_recv), (dy, j), c_peer)

    forward(0)
    for event in ARRIVALS:
        if event[0] == "z":
            arrived(place(rows, 0, *unit(event[1])), z_recv.at[event[1]])
            forward(event[1])
        else:
            along_y[event[1:]].wait_recv()
            share(*event[1:])
    for d in (1, 3, 2):
        for i in range(4):
            arrived(cols.at[(r - d) % 4, i], x_recv.at[d, i])
    for copy in across.values():
        copy.wait_recv()
    for d in (0, 2, 6, 4):
        at = ((z - d) % 8) // 2
        cols[r, at] = rows[y, zl, core, at]
    for copy in started:
        copy.wait_send()
    for d in (1, 3, 2):
        for slot in range(4):
            to_columns(0, d, slot).wait_send()


def correlate(rows, cols, out, left, right, stage, out_sem):
    lane = lax.broadcasted_iota(jnp.int32, (256, 128), 1)
    long_lane = lax.broadcasted_iota(jnp.int32, (1024, 128), 1)
    real_lane = (lane & 1) == 0

    def write(channel, part):
        return pltpu.make_async_copy(stage.at[channel, part], out.at[channel, part], out_sem.at[channel, part])

    for c_hi in range(2):
        x = rows[:, :, :, :, c_hi].reshape(1024, 128)
        turned = pltpu.roll(x, 64, 1)
        high = x.astype(jnp.bfloat16)
        left[c_hi, 0] = jnp.where(long_lane < 64, x, turned).astype(jnp.bfloat16)
        left[c_hi, 1] = jnp.where(long_lane < 64, turned, x).astype(jnp.bfloat16)
        left[c_hi, 2] = (x - high.astype(jnp.float32)).astype(jnp.bfloat16)
        c = cols[:, :, c_hi].reshape(256, 128) * (1.0 / SPEC)
        c_turned = pltpu.roll(c, 64, 1)
        for p in range(2):
            mine = (lane >> 6) == p
            operand = jnp.concatenate([left[c_hi, p], left[c_hi, 2]], axis=1)
            straight = jnp.where(mine, c, c_turned)
            swapped = jnp.where(real_lane, -pltpu.roll(straight, 127, 1), pltpu.roll(straight, 1, 1))
            for part, value in enumerate((straight, swapped)):
                value_high = value.astype(jnp.bfloat16).astype(jnp.float32)
                first = jnp.where(lane < 64, value_high, value - value_high)
                second = jnp.where(mine, value_high, 0.0)
                for e in range(2):
                    mask = ((lane >> 1) & 1) == e
                    channel = c_hi * 4 + p * 2 + e
                    right[channel, part] = jnp.concatenate(
                        [jnp.where(mask, first, 0.0), jnp.where(mask, second, 0.0)], axis=1
                    ).astype(jnp.bfloat16)
                    stage[channel, part] = lax.dot_general(
                        operand, right[channel, part], NT, preferred_element_type=jnp.float32
                    ).astype(jnp.bfloat16)
                    write(channel, part).start()
    for channel in range(8):
        for part in range(2):
            write(channel, part).wait()


def shards(samples, kept_channels, flags):
    vmem = pl.BlockSpec(memory_space=pltpu.VMEM)
    hbm = pl.BlockSpec(memory_space=pltpu.HBM)
    dma = pltpu.SemaphoreType.DMA
    rows, cols = pl.pallas_call(
        spread,
        out_shape=[pltpu.VMEM((4, 2, 2, 4, 2, 16, 128), jnp.float32), pltpu.VMEM((4, 4, 2, 16, 128), jnp.float32)],
        in_specs=[hbm, hbm, hbm],
        out_specs=[vmem, vmem],
        scratch_shapes=[
            pltpu.VMEM((CHUNKS, BLOCKS, 16, CHUNK), jnp.int32),
            pltpu.VMEM((BLOCKS * 16, NFFT), jnp.bfloat16),
            pltpu.VMEM((512, NFFT), jnp.bfloat16),
            pltpu.VMEM((128, 128), jnp.float32),
            pltpu.VMEM((4, 2, 16, 128), jnp.float32),
            pltpu.SMEM((32,), jnp.int32),
            pltpu.SMEM((16,), jnp.int32),
            dma((CHUNKS,)),
            dma((2,)),
            dma((8,)),
            dma((8,)),
            dma((4, 8)),
            dma((4, 8)),
            dma((4, 8)),
            dma((4, 8)),
            dma((4, 4)),
            dma((4, 4)),
        ],
        compiler_params=pltpu.CompilerParams(
            collective_id=0, has_side_effects=True, vmem_limit_bytes=40 * 1024 * 1024
        ),
        name="spread",
    )(*[pltpu.with_memory_space_constraint(array, pltpu.HBM) for array in (samples, kept_channels, flags)])
    return pl.pallas_call(
        correlate,
        out_shape=jax.ShapeDtypeStruct((8, 2, 1024, 256), jnp.bfloat16),
        in_specs=[vmem, vmem],
        out_specs=hbm,
        scratch_shapes=[
            pltpu.VMEM((2, 3, 1024, 128), jnp.bfloat16),
            pltpu.VMEM((8, 2, 256, 256), jnp.bfloat16),
            pltpu.VMEM((8, 2, 1024, 256), jnp.bfloat16),
            dma((8, 2)),
        ],
        compiler_params=pltpu.CompilerParams(vmem_limit_bytes=40 * 1024 * 1024),
        name="correlate",
    )(rows, cols)


def solution(mesh):
    return jax.shard_map(
        shards,
        mesh=mesh,
        in_specs=(P(("xr", "xc", "af"), None), P(), P(("xr", "xc", "af"))),
        out_specs=P("af", None, "xr", "xc"),
        check_vma=False,
    )
```

time: 39.3 us -> 30 us (0.76)
  Pallas kernels: 35.5 us -> 29.9 us
  local copies, waits for them, and re-layouts: 3.72 us -> 0 us
    pallas_call x1, Pallas kernels: 30.5 us -> 25.9 us  [shards(): pl.pallas_call(spread, out_shape=[pltpu.VMEM((4, 2, 2, 4, 2, 16, 128), jn...]
    unnamed x6 -> x0, local copies, waits for them, and re-layouts: 3.72 us -> none
    pallas_call x1, Pallas kernels: 4.92 us -> 4.05 us  [shards(): pl.pallas_call(correlate, out_shape=jax.ShapeDtypeStruct((8, 2, 1024, 256...]
where the time goes in v2:
time: 30 us; the launch traced here: 29.9 us
  Pallas kernels  29.9 us (100%)
    pallas_call x1, Pallas kernels, shards(): pl.pallas_call(spread, out_shape=[pltpu.VMEM((4, 2, 2, 4, 2, 16, 128), jn...  25.9 us
    pallas_call x1, Pallas kernels, shards(): pl.pallas_call(correlate, out_shape=jax.ShapeDtypeStruct((8, 2, 1024, 256...  4.05 us

profile of v2, /device:TPU:1, one launch (start us, length us, event | category | flops | bytes accessed | tf_op | source)
XLA Modules:
  0.0 29.9 jit_solution(8105877767036592357)
XLA Ops:
  0.0 25.9 %spread.1 = (f32[4,2,2,4,2,16,128]{6,5,4,3,2,1,0:T(8,128)S(1)}, f32[4,4,2,16,128]{4,3,2,1,0:T(8,128)S(1)}) custom-call(s32[16,77824]{1,0:T(8,128)} %samples.1, s32[32]{0:T(128)} %kept_hbm.1, s32[16]{0:T(128)} %flags_hbm.1), custom_call_target="tpu_custom_call" | custom-call | tf_op jit(solution)/shard_map/spread/pallas_call | solution.py:308
  25.9 4.1 %correlate.1 = bf16[8,2,1024,256]{3,2,1,0:T(8,128)(2,1)} custom-call(f32[4,2,2,4,2,16,128]{6,5,4,3,2,1,0:T(8,128)S(1)} %get-tuple-element.7.rows, f32[4,4,2,16,128]{4,3,2,1,0:T(8,128)S(1)} %get-tuple-element.8.cols), custom_call_target="tpu_custom_call" | custom-call | tf_op jit(solution)/shard_map/correlate/pallas_call | solution.py:337

commit v3 on v2

--- a/solution.py
+++ b/solution.py
@@ -22,8 +22,8 @@
 )
 Z_ORDER = (4, 3, 5, 2, 6, 1, 7)
 ARRIVALS = (
-    ("z", 1), ("z", 2), ("y", 1, 0), ("y", 3, 0), ("z", 3), ("z", 4), ("y", 2, 0), ("z", 5), ("z", 6), ("z", 7),
-    *(("y", dy, j) for j in range(1, 8) for dy in (1, 3, 2)),
+    ("z", 1), ("z", 2), ("near", 0), ("z", 3), ("z", 4), ("far", 0), ("z", 5), ("z", 6), ("z", 7),
+    *((kind, j) for j in range(1, 8) for kind in ("near", "far")),
 )
 
 
@@ -49,7 +49,7 @@
     load_sem, small_sem, z_send, z_recv, y_send, y_recv, c_send, c_recv, x_send, x_recv,
 ):
     f, r, k = lax.axis_index("af"), lax.axis_index("xr"), lax.axis_index("xc")
-    y, zl, core = k // 4, (k // 2) % 2, k % 2
+    y, zl, core = lax.div(k, 4), lax.rem(lax.div(k, 2), 2), lax.rem(k, 2)
     z = f * 2 + zl
 
     small = [
@@ -68,14 +68,14 @@
         return pair[0] if pair[0] == pair[1] else pair[0] + core * (pair[1] - pair[0])
 
     def on_z(d, cc):
-        zz = (z + d) % 8
-        return {"af": zz // 2, "xc": y * 4 + (zz % 2) * 2 + cc}
-
-    y_peers = {d: {"xc": ((y + d) % 4) * 4 + zl * 2 + core} for d in (1, 3, 2)}
+        zz = lax.rem(z + d, 8)
+        return {"af": lax.div(zz, 2), "xc": y * 4 + lax.rem(zz, 2) * 2 + cc}
+
+    y_peers = {d: {"xc": lax.rem(y + d, 4) * 4 + zl * 2 + core} for d in (1, 3, 2)}
     c_peer = {"xc": k + 1 - 2 * core}
 
     def on_x(d, cc):
-        return {"xr": (r + d) % 4, "xc": y * 4 + zl * 2 + cc}
+        return {"xr": lax.rem(r + d, 4), "xc": y * 4 + zl * 2 + cc}
 
     barrier = pltpu.get_barrier_semaphore()
     greeted = [on_z(d, cc) for d in range(1, 8) for cc in range(2)] + [on_x(d, cc) for d in range(1, 4) for cc in range(2)]
@@ -158,106 +158,85 @@
 
     pl.semaphore_wait(barrier, len(greeted))
 
-    started = []
-
-    def copy_to(src, dst, sems, send_at, recv_at, peer):
-        return pltpu.make_async_remote_copy(
+    def send(src, dst, send_sem, recv_sem, peer):
+        pltpu.make_async_remote_copy(
             src_ref=src,
             dst_ref=dst,
-            send_sem=sems[0].at[send_at],
-            recv_sem=sems[1].at[recv_at],
+            send_sem=send_sem,
+            recv_sem=recv_sem,
             device_id=peer,
             device_id_type=MESH,
-        )
-
-    def send(src, dst, sems, at, peer):
-        copy = copy_to(src, dst, sems, at, at, peer)
-        copy.start()
-        started.append(copy)
-        return copy
-
-    def arrived(block, sem):
-        pltpu.make_async_copy(block, block, sem).wait()
+        ).start()
+
+    def done(ref, sem):
+        pltpu.make_async_copy(ref, ref, sem).wait()
 
     def place(ref, dy, dz, cc):
-        yy, zz = (y - dy) % 4, (z - dz) % 8
-        return ref.at[yy, zz % 2, cc, zz // 2]
+        yy, zz = lax.rem(y + 4 - dy, 4), lax.rem(z + 8 - dz, 8)
+        return ref.at[yy, lax.rem(zz, 2), cc, lax.div(zz, 2)]
 
     def unit(j):
         return tuple(pick((UNITS[0][j][n], UNITS[1][j][n])) for n in range(2))
 
-    along_y, across = {}, {}
     mine = place(rows, 0, 0, core)
     for d in Z_ORDER:
         hosts = [next((cc, j) for cc in range(2) for j in range(8) if UNITS[cc][j] == (d, source)) for source in range(2)]
-        copy = copy_to(
-            blocks.at[((z + d) % 8) // 2],
+        send(
+            blocks.at[lax.div(lax.rem(z + d, 8), 2)],
             mine,
-            (z_send, z_recv),
-            (d,),
-            (pick((hosts[0][1], hosts[1][1])),),
+            z_send,
+            z_recv.at[pick((hosts[0][1], hosts[1][1]))],
             on_z(d, pick((hosts[0][0], hosts[1][0]))),
         )
-        copy.start()
-        started.append(copy)
     mine[...] = blocks[f]
 
-    def to_columns(j, d, slot):
+    def to_columns(j):
         dz, source = unit(j)
-        return copy_to(
-            place(rows, 0, dz, source),
-            cols.at[r, ((z - dz) % 8) // 2],
-            (x_send, x_recv),
-            (d, slot),
-            (d, dz // 2),
-            on_x(d, source),
-        )
+        for d in (1, 3, 2):
+            send(
+                place(rows, 0, dz, source),
+                cols.at[r, lax.div(lax.rem(z + 8 - dz, 8), 2)],
+                x_send,
+                x_recv,
+                on_x(d, source),
+            )
 
     def forward(j):
         block = place(rows, 0, *unit(j))
         for d, peer in y_peers.items():
-            along_y[d, j] = send(block, block, (y_send, y_recv), (d, j), peer)
-        slots = [
-            [i for i in range(8) if UNITS[cc][i][0] % 2 == 0].index(j) if UNITS[cc][j][0] % 2 == 0 else None
-            for cc in range(2)
-        ]
-        for d in (1, 3, 2):
-            if slots[0] == slots[1] and slots[0] is not None:
-                to_columns(j, d, slots[0]).start()
-            elif slots != [None, None]:
-                owner = 0 if slots[1] is None else 1
-
-                @pl.when(core == owner)
-                def _():
-                    to_columns(j, d, slots[owner]).start()
-
+            send(block, block, y_send, y_recv.at[1 if d == 2 else 0, j], peer)
+        even = [UNITS[cc][j][0] % 2 == 0 for cc in range(2)]
+        if all(even):
+            to_columns(j)
+        elif any(even):
+            pl.when(core == even.index(True))(lambda: to_columns(j))
         share(0, j)
 
     def share(dy, j):
         block = place(rows, dy, *unit(j))
-        across[dy, j] = send(block, block, (c_send, c_recv), (dy, j), c_peer)
+        send(block, block, c_send, c_recv, c_peer)
 
     forward(0)
-    for event in ARRIVALS:
-        if event[0] == "z":
-            arrived(place(rows, 0, *unit(event[1])), z_recv.at[event[1]])
-            forward(event[1])
+    for kind, j in ARRIVALS:
+        if kind == "z":
+            done(place(rows, 0, *unit(j)), z_recv.at[j])
+            forward(j)
+        elif kind == "near":
+            done(raw.at[0, 0:2, :, 0:256], y_recv.at[0, j])
+            share(1, j)
+            share(3, j)
         else:
-            along_y[event[1:]].wait_recv()
-            share(*event[1:])
-    for d in (1, 3, 2):
-        for i in range(4):
-            arrived(cols.at[(r - d) % 4, i], x_recv.at[d, i])
-    for copy in across.values():
-        copy.wait_recv()
+            done(raw.at[0, 0:1, :, 0:256], y_recv.at[1, j])
+            share(2, j)
+    done(raw.at[0, 0:3], x_recv)
+    done(raw.at[0, 0:8], c_recv)
     for d in (0, 2, 6, 4):
-        at = ((z - d) % 8) // 2
+        at = lax.div(lax.rem(z + 8 - d, 8), 2)
         cols[r, at] = rows[y, zl, core, at]
-    for copy in started:
-        copy.wait_send()
-    for d in (1, 3, 2):
-        for slot in range(4):
-            to_columns(0, d, slot).wait_send()
+    done(raw.at[0, 0:7, :, 0:256], z_send)
+    done(raw.at[0, 0:6], y_send)
+    done(raw.at[0, 0:3], x_send)
+    done(raw.at[0, 0:8], c_send)
 
 
 def correlate(rows, cols, out, left, right, stage, out_sem):
@@ -266,7 +245,7 @@
     real_lane = (lane & 1) == 0
 
     def write(channel, part):
-        return pltpu.make_async_copy(stage.at[channel, part], out.at[channel, part], out_sem.at[channel, part])
+        return pltpu.make_async_copy(stage.at[channel, part], out.at[channel, part], out_sem)
 
     for c_hi in range(2):
         x = rows[:, :, :, :, c_hi].reshape(1024, 128)
@@ -296,9 +275,7 @@
                         operand, right[channel, part], NT, preferred_element_type=jnp.float32
                     ).astype(jnp.bfloat16)
                     write(channel, part).start()
-    for channel in range(8):
-        for part in range(2):
-            write(channel, part).wait()
+    pltpu.make_async_copy(stage, out, out_sem).wait()
 
 
 def shards(samples, kept_channels, flags):
@@ -320,14 +297,14 @@
             pltpu.SMEM((16,), jnp.int32),
             dma((CHUNKS,)),
             dma((2,)),
+            dma,
             dma((8,)),
-            dma((8,)),
-            dma((4, 8)),
-            dma((4, 8)),
-            dma((4, 8)),
-            dma((4, 8)),
-            dma((4, 4)),
-            dma((4, 4)),
+            dma,
+            dma((2, 8)),
+            dma,
+            dma,
+            dma,
+            dma,
         ],
         compiler_params=pltpu.CompilerParams(
             collective_id=0, has_side_effects=True, vmem_limit_bytes=40 * 1024 * 1024
@@ -343,7 +320,7 @@
             pltpu.VMEM((2, 3, 1024, 128), jnp.bfloat16),
             pltpu.VMEM((8, 2, 256, 256), jnp.bfloat16),
             pltpu.VMEM((8, 2, 1024, 256), jnp.bfloat16),
-            dma((8, 2)),
+            dma,
         ],
         compiler_params=pltpu.CompilerParams(vmem_limit_bytes=40 * 1024 * 1024),
         name="correlate",

time: 30 us -> 28.5 us (0.950)
  Pallas kernels: 29.9 us -> 28.4 us
    pallas_call x1, Pallas kernels: 25.9 us -> 24.4 us  [shards(): pl.pallas_call(spread, out_shape=[pltpu.VMEM((4, 2, 2, 4, 2, 16, 128), jn...]
where the time goes in v3:
time: 28.5 us; the launch traced here: 28.4 us
  Pallas kernels  28.4 us (100%)
    pallas_call x1, Pallas kernels, shards(): pl.pallas_call(spread, out_shape=[pltpu.VMEM((4, 2, 2, 4, 2, 16, 128), jn...  24.4 us
    pallas_call x1, Pallas kernels, shards(): pl.pallas_call(correlate, out_shape=jax.ShapeDtypeStruct((8, 2, 1024, 256...  3.93 us

profile of v3, /device:TPU:1, one launch (start us, length us, event | category | flops | bytes accessed | tf_op | source)
XLA Modules:
  0.0 28.4 jit_solution(8175444697258403806)
XLA Ops:
  0.0 24.4 %spread.1 = (f32[4,2,2,4,2,16,128]{6,5,4,3,2,1,0:T(8,128)S(1)}, f32[4,4,2,16,128]{4,3,2,1,0:T(8,128)S(1)}) custom-call(s32[16,77824]{1,0:T(8,128)} %samples.1, s32[32]{0:T(128)} %kept_hbm.1, s32[16]{0:T(128)} %flags_hbm.1), custom_call_target="tpu_custom_call" | custom-call | tf_op jit(solution)/shard_map/spread/pallas_call | solution.py:285
  24.4 3.9 %correlate.1 = bf16[8,2,1024,256]{3,2,1,0:T(8,128)(2,1)} custom-call(f32[4,2,2,4,2,16,128]{6,5,4,3,2,1,0:T(8,128)S(1)} %get-tuple-element.7.rows, f32[4,4,2,16,128]{4,3,2,1,0:T(8,128)S(1)} %get-tuple-element.8.cols), custom_call_target="tpu_custom_call" | custom-call | tf_op jit(solution)/shard_map/correlate/pallas_call | solution.py:314

commit v4 on v3

--- a/solution.py
+++ b/solution.py
@@ -17,13 +17,14 @@
 MESH = pl.DeviceIdType.MESH
 NT = (((1,), (1,)), ((), ()))
 UNITS = (
-    ((0, 0), (1, 1), (7, 1), (1, 0), (7, 0), (6, 1), (6, 0), (2, 0)),
-    ((0, 1), (2, 1), (3, 1), (5, 1), (3, 0), (5, 0), (4, 1), (4, 0)),
+    ((0, 0), (7, 1), (1, 0), (7, 0), (6, 1), (2, 1), (6, 0), (2, 0)),
+    ((0, 1), (1, 1), (3, 1), (5, 1), (3, 0), (5, 0), (4, 1), (4, 0)),
 )
+DIRECT = (1, 7)
 Z_ORDER = (4, 3, 5, 2, 6, 1, 7)
 ARRIVALS = (
-    ("z", 1), ("z", 2), ("near", 0), ("z", 3), ("z", 4), ("far", 0), ("z", 5), ("z", 6), ("z", 7),
-    *((kind, j) for j in range(1, 8) for kind in ("near", "far")),
+    ("pass", 0), *(("z", j) for j in range(1, 8)), *(("pass", j) for j in (6, 7, 4, 5, 1, 2, 3)),
+    *((kind, j) for j in range(8) for kind in ("near", "far")),
 )
 
 
@@ -80,6 +81,11 @@
     barrier = pltpu.get_barrier_semaphore()
     greeted = [on_z(d, cc) for d in range(1, 8) for cc in range(2)] + [on_x(d, cc) for d in range(1, 4) for cc in range(2)]
     greeted += [*y_peers.values(), c_peer]
+    for d in DIRECT:
+        for cc in range(2):
+            for dy in (1, 2, 3):
+                peer = on_z(d, cc)
+                greeted.append({**peer, "xc": peer["xc"] - y * 4 + lax.rem(y + dy, 4) * 4})
     for peer in greeted:
         pl.semaphore_signal(barrier, inc=1, device_id=peer, device_id_type=MESH)
 
@@ -171,14 +177,23 @@
     def done(ref, sem):
         pltpu.make_async_copy(ref, ref, sem).wait()
 
-    def place(ref, dy, dz, cc):
-        yy, zz = lax.rem(y + 4 - dy, 4), lax.rem(z + 8 - dz, 8)
-        return ref.at[yy, lax.rem(zz, 2), cc, lax.div(zz, 2)]
-
-    def unit(j):
-        return tuple(pick((UNITS[0][j][n], UNITS[1][j][n])) for n in range(2))
-
-    mine = place(rows, 0, 0, core)
+    def done_blocks(counts, sem):
+        for cc, count in enumerate(counts):
+            width = max(n for n in range(1, 5) if count % n == 0)
+            like = raw.at[0, 0 : count // width, :, 0 : 256 * width]
+            if counts[0] == counts[1]:
+                return done(like, sem)
+            pl.when(core == cc)(functools.partial(done, like, sem))
+
+    units = [tuple(pick((UNITS[0][j][n], UNITS[1][j][n])) for n in range(2)) for j in range(8)]
+    spots = [lax.rem(z + 8 - dz, 8) for dz, _ in units]
+    spots = [(lax.rem(zz, 2), source, lax.div(zz, 2)) for zz, (_, source) in zip(spots, units)]
+    lines = [lax.rem(y + 4 - dy, 4) for dy in range(4)]
+
+    def place(dy, j):
+        return rows.at[(lines[dy], *spots[j])]
+
+    mine = rows.at[y, zl, core, f]
     for d in Z_ORDER:
         hosts = [next((cc, j) for cc in range(2) for j in range(8) if UNITS[cc][j] == (d, source)) for source in range(2)]
         send(
@@ -188,39 +203,47 @@
             z_recv.at[pick((hosts[0][1], hosts[1][1]))],
             on_z(d, pick((hosts[0][0], hosts[1][0]))),
         )
+    for d in DIRECT:
+        hosts = [next((cc, j) for cc in range(2) for j in range(8) if UNITS[cc][j] == (d, source)) for source in range(2)]
+        host, j = pick((hosts[0][0], hosts[1][0])), pick((hosts[0][1], hosts[1][1]))
+        for dy in (2, 1, 3):
+            peer = on_z(d, host)
+            peer["xc"] = peer["xc"] - y * 4 + lax.rem(y + dy, 4) * 4
+            send(blocks.at[lax.div(lax.rem(z + d, 8), 2)], mine, z_send, y_recv.at[1 if dy == 2 else 0, j], peer)
     mine[...] = blocks[f]
 
     def to_columns(j):
-        dz, source = unit(j)
         for d in (1, 3, 2):
-            send(
-                place(rows, 0, dz, source),
-                cols.at[r, lax.div(lax.rem(z + 8 - dz, 8), 2)],
-                x_send,
-                x_recv,
-                on_x(d, source),
-            )
+            send(place(0, j), cols.at[r, spots[j][2]], x_send, x_recv, on_x(d, spots[j][1]))
+
+    def where(j, test, act):
+        passed = [test(UNITS[cc][j][0]) for cc in range(2)]
+        if all(passed):
+            act()
+        elif any(passed):
+            pl.when(core == passed.index(True))(act)
 
     def forward(j):
-        block = place(rows, 0, *unit(j))
-        for d, peer in y_peers.items():
-            send(block, block, y_send, y_recv.at[1 if d == 2 else 0, j], peer)
-        even = [UNITS[cc][j][0] % 2 == 0 for cc in range(2)]
-        if all(even):
-            to_columns(j)
-        elif any(even):
-            pl.when(core == even.index(True))(lambda: to_columns(j))
-        share(0, j)
+        block = place(0, j)
+
+        def to_rows():
+            for d, peer in y_peers.items():
+                send(block, block, y_send, y_recv.at[1 if d == 2 else 0, j], peer)
+
+        where(j, lambda dz: dz not in DIRECT, to_rows)
 
     def share(dy, j):
-        block = place(rows, dy, *unit(j))
+        block = place(dy, j)
         send(block, block, c_send, c_recv, c_peer)
 
     forward(0)
     for kind, j in ARRIVALS:
         if kind == "z":
-            done(place(rows, 0, *unit(j)), z_recv.at[j])
+            done(place(0, j), z_recv.at[j])
             forward(j)
+        elif kind == "pass":
+            where(j, lambda dz: dz % 2 == 0, lambda: to_columns(j))
+            share(0, j)
         elif kind == "near":
             done(raw.at[0, 0:2, :, 0:256], y_recv.at[0, j])
             share(1, j)
@@ -228,15 +251,15 @@
         else:
             done(raw.at[0, 0:1, :, 0:256], y_recv.at[1, j])
             share(2, j)
-    done(raw.at[0, 0:3], x_recv)
-    done(raw.at[0, 0:8], c_recv)
+    done_blocks((12, 12), x_recv)
+    done_blocks((32, 32), c_recv)
     for d in (0, 2, 6, 4):
         at = lax.div(lax.rem(z + 8 - d, 8), 2)
         cols[r, at] = rows[y, zl, core, at]
-    done(raw.at[0, 0:7, :, 0:256], z_send)
-    done(raw.at[0, 0:6], y_send)
-    done(raw.at[0, 0:3], x_send)
-    done(raw.at[0, 0:8], c_send)
+    done_blocks((7 + 3 * len(DIRECT),) * 2, z_send)
+    done_blocks([3 * sum(dz not in DIRECT for dz, _ in units) for units in UNITS], y_send)
+    done_blocks([3 * sum(dz % 2 == 0 for dz, _ in units) for units in UNITS], x_send)
+    done_blocks((32, 32), c_send)
 
 
 def correlate(rows, cols, out, left, right, stage, out_sem):

time: 28.5 us -> 28.1 us (0.986)
  Pallas kernels: 28.4 us -> 28 us
    pallas_call x1, Pallas kernels: 24.4 us -> 24.1 us  [shards(): pl.pallas_call(spread, out_shape=[pltpu.VMEM((4, 2, 2, 4, 2, 16, 128), jn...]
where the time goes in v4:
time: 28.1 us; the launch traced here: 28 us
  Pallas kernels  28 us (100%)
    pallas_call x1, Pallas kernels, shards(): pl.pallas_call(spread, out_shape=[pltpu.VMEM((4, 2, 2, 4, 2, 16, 128), jn...  24.1 us
    pallas_call x1, Pallas kernels, shards(): pl.pallas_call(correlate, out_shape=jax.ShapeDtypeStruct((8, 2, 1024, 256...  3.94 us

profile of v4, /device:TPU:1, one launch (start us, length us, event | category | flops | bytes accessed | tf_op | source)
XLA Modules:
  0.0 28.0 jit_solution(17426676482332859901)
XLA Ops:
  0.0 24.1 %spread.1 = (f32[4,2,2,4,2,16,128]{6,5,4,3,2,1,0:T(8,128)S(1)}, f32[4,4,2,16,128]{4,3,2,1,0:T(8,128)S(1)}) custom-call(s32[16,77824]{1,0:T(8,128)} %samples.1, s32[32]{0:T(128)} %kept_hbm.1, s32[16]{0:T(128)} %flags_hbm.1), custom_call_target="tpu_custom_call" | custom-call | tf_op jit(solution)/shard_map/spread/pallas_call | solution.py:308
  24.1 3.9 %correlate.1 = bf16[8,2,1024,256]{3,2,1,0:T(8,128)(2,1)} custom-call(f32[4,2,2,4,2,16,128]{6,5,4,3,2,1,0:T(8,128)S(1)} %get-tuple-element.7.rows, f32[4,4,2,16,128]{4,3,2,1,0:T(8,128)S(1)} %get-tuple-element.8.cols), custom_call_target="tpu_custom_call" | custom-call | tf_op jit(solution)/shard_map/correlate/pallas_call | solution.py:337

commit v5 on v4

--- a/solution.py
+++ b/solution.py
@@ -13,6 +13,7 @@
 SPEC = 16
 BLOCKS = SPEC + TAPS - 1
 CHUNKS = 4
+EARLY = 0
 CHUNK = NFFT // CHUNKS
 MESH = pl.DeviceIdType.MESH
 NT = (((1,), (1,)), ((), ()))
@@ -20,8 +21,9 @@
     ((0, 0), (7, 1), (1, 0), (7, 0), (6, 1), (2, 1), (6, 0), (2, 0)),
     ((0, 1), (1, 1), (3, 1), (5, 1), (3, 0), (5, 0), (4, 1), (4, 0)),
 )
-DIRECT = (1, 7)
-Z_ORDER = (4, 3, 5, 2, 6, 1, 7)
+DIRECT = {1: (2, 1, 3), 7: (2, 1, 3), 2: (2,), 6: (2,)}
+HALVES = ((4, 3, 5), (2, 6, 1, 7))
+SLOTS = {4: (0, 0), 3: (1, 0), 5: (0, 1), 2: (1, 2), 6: (2, 1), 1: (3, 2), 7: (2, 3)}
 ARRIVALS = (
     ("pass", 0), *(("z", j) for j in range(1, 8)), *(("pass", j) for j in (6, 7, 4, 5, 1, 2, 3)),
     *((kind, j) for j in range(8) for kind in ("near", "far")),
@@ -81,9 +83,9 @@
     barrier = pltpu.get_barrier_semaphore()
     greeted = [on_z(d, cc) for d in range(1, 8) for cc in range(2)] + [on_x(d, cc) for d in range(1, 4) for cc in range(2)]
     greeted += [*y_peers.values(), c_peer]
-    for d in DIRECT:
+    for d in sorted({*DIRECT, *(8 - d for d in DIRECT)}):
         for cc in range(2):
-            for dy in (1, 2, 3):
+            for dy in sorted({*DIRECT.get(d, ()), *(4 - dy for dy in DIRECT.get(8 - d, ()))}):
                 peer = on_z(d, cc)
                 greeted.append({**peer, "xc": peer["xc"] - y * 4 + lax.rem(y + dy, 4) * 4})
     for peer in greeted:
@@ -104,7 +106,9 @@
 
     lane = lax.broadcasted_iota(jnp.int32, (64, 128), 1)
     line = lax.broadcasted_iota(jnp.int32, (64, 128), 0)
-    channel = ((line >> 2) & 7) * 4 + (line >> 5) * 2 + ((line >> 1) & 1)
+    slot = line >> 5 << 1 | ((line >> 3) & 1)
+    ahead = jnp.where(slot == 0, 2, jnp.where(slot == 1, 1 + 2 * zl, jnp.where(slot == 2, 3 - 2 * zl, 0)))
+    channel = ((f + ahead) & 3) * 8 + ((line >> 2) & 1) * 4 + ((line >> 4) & 1) * 2 + ((line >> 1) & 1)
     kept_line = jnp.zeros((64, 128), jnp.int32)
     for j in range(32):
         kept_line = jnp.where(channel == j, kept[j], kept_line)
@@ -112,7 +116,12 @@
     coarse_s, coarse_c = sincos((kept_line * (128 * (lane & 31)) + quarter_turn) & (NFFT - 1), NFFT)
     fine_s, fine_c = sincos((kept_line * lane) & (NFFT - 1), NFFT)
 
-    summed = None
+    def multiply(half, span):
+        return lax.dot_general(
+            frames[:, span], table[half * 256 : half * 256 + 256, span], NT, preferred_element_type=jnp.float32
+        )
+
+    partial = [0.0, 0.0]
     for part in range(CHUNKS):
         for a in range(part * CHUNK // 128, (part + 1) * CHUNK // 128):
             trig = coarse_c[:, a : a + 1] * fine_c - coarse_s[:, a : a + 1] * fine_s
@@ -120,47 +129,57 @@
                 value = trig * window[t * 32 + a : t * 32 + a + 1, :]
                 high = value.astype(jnp.bfloat16)
                 low = (value - high.astype(jnp.float32)).astype(jnp.bfloat16)
-                for half in range(2):
-                    at = (t // 2) * 128 + half * 64 + (t % 2) * 32
-                    table[at : at + 32, a * 128 : (a + 1) * 128] = high[half * 32 : half * 32 + 32]
-                    table[256 + at : 256 + at + 32, a * 128 : (a + 1) * 128] = low[half * 32 : half * 32 + 32]
+                for quarter in range(4):
+                    at = quarter // 2 * 256 + quarter % 2 * 64 + t * 16
+                    table[at : at + 16, a * 128 : (a + 1) * 128] = high[quarter * 16 : quarter * 16 + 16]
+                    table[at + 128 : at + 144, a * 128 : (a + 1) * 128] = low[quarter * 16 : quarter * 16 + 16]
         pltpu.make_async_copy(raw.at[part], raw.at[part], load_sem.at[part]).wait()
         span = slice(part * CHUNK, (part + 1) * CHUNK)
         for b in range(BLOCKS):
             frames[b * 16 : (b + 1) * 16, span] = raw[part, b].astype(jnp.float32).astype(jnp.bfloat16)
-        product = lax.dot_general(frames[:, span], table[:, span], NT, preferred_element_type=jnp.float32)
-        summed = product if summed is None else summed + product
-
-    summed = summed[:, :256] + summed[:, 256:]
-    first, second = summed[:, :128], summed[:, 128:]
-    wide_lane = lax.broadcasted_iota(jnp.int32, (256, 128), 1)
-    tapped = jnp.where(
-        (wide_lane & 32) == 0, first[0:256] + second[32:288], first[16:272] + second[48:304]
-    )
-    lane = lax.broadcasted_iota(jnp.int32, (128, 128), 1)
-    low_tap = (lane & 32) == 0
-    early, late = tapped[:128], tapped[128:]
-    crossed = jnp.where(low_tap, late, early)
-    crossed = jnp.where(low_tap, pltpu.roll(crossed, 96, 1), pltpu.roll(crossed, 32, 1))
-    both = jnp.where(low_tap, early, late) + crossed
-    tiles = [both[16 * j : 16 * j + 16] for j in range(8)]
-    lane = lax.broadcasted_iota(jnp.int32, (16, 128), 1)
-    for bit in range(3):
-        step = 4 << bit
-        low_lane = (lane & step) == 0
-        for j in range(8):
-            if j & (1 << bit):
-                continue
-            zero, one = tiles[j], tiles[j | (1 << bit)]
-            tiles[j] = jnp.where(low_lane, zero, pltpu.roll(one, step, 1))
-            tiles[j | (1 << bit)] = jnp.where(low_lane, pltpu.roll(zero, 128 - step, 1), one)
+        if part < EARLY:
+            continue
+        span = slice(0 if part == EARLY else part * CHUNK, (part + 1) * CHUNK)
+        for half in range(2 if part < CHUNKS - 1 else 1):
+            partial[half] = partial[half] + multiply(half, span)
+
     row = lax.broadcasted_iota(jnp.int32, (16, 128), 0)
     gain = jnp.zeros((16, 128), jnp.int32)
     for j in range(16):
         gain = jnp.where(row == j, flags[j], gain)
     gain = gain.astype(jnp.float32) * scale
-    for j in range(8):
-        blocks[j // 2, j % 2] = tiles[j] * gain
+
+    def gather(half, product):
+        product = product[:, :128] + product[:, 128:]
+        lane = lax.broadcasted_iota(jnp.int32, (256, 128), 1)
+        tap = (lane >> 4) & 3
+        both = jnp.where(
+            tap < 2,
+            jnp.where(tap == 0, product[0:256], product[16:272]),
+            jnp.where(tap == 2, product[32:288], product[48:304]),
+        )
+        for step in (32, 16):
+            count = both.shape[0] // 2
+            zero = (lax.broadcasted_iota(jnp.int32, (count, 128), 1) & step) == 0
+            first, second = both[:count], both[count:]
+            crossed = jnp.where(zero, second, first)
+            crossed = jnp.where(zero, pltpu.roll(crossed, 128 - step, 1), pltpu.roll(crossed, step, 1))
+            both = jnp.where(zero, first, second) + crossed
+        tiles = [both[16 * j : 16 * j + 16] for j in range(4)]
+        lane = lax.broadcasted_iota(jnp.int32, (16, 128), 1)
+        for bit in range(2):
+            step = 4 << bit
+            zero = (lane & step) == 0
+            for j in range(4):
+                if j & (1 << bit):
+                    continue
+                first, second = tiles[j], tiles[j | (1 << bit)]
+                tiles[j] = jnp.where(zero, first, pltpu.roll(second, step, 1))
+                tiles[j | (1 << bit)] = jnp.where(zero, pltpu.roll(first, 128 - step, 1), second)
+        for j in range(4):
+            blocks[half * 2 + j // 2, j % 2] = tiles[j] * gain
+
+    gather(0, partial[0])
 
     pl.semaphore_wait(barrier, len(greeted))
 
@@ -194,23 +213,23 @@
         return rows.at[(lines[dy], *spots[j])]
 
     mine = rows.at[y, zl, core, f]
-    for d in Z_ORDER:
-        hosts = [next((cc, j) for cc in range(2) for j in range(8) if UNITS[cc][j] == (d, source)) for source in range(2)]
-        send(
-            blocks.at[lax.div(lax.rem(z + d, 8), 2)],
-            mine,
-            z_send,
-            z_recv.at[pick((hosts[0][1], hosts[1][1]))],
-            on_z(d, pick((hosts[0][0], hosts[1][0]))),
-        )
-    for d in DIRECT:
+
+    def hand_out(d):
         hosts = [next((cc, j) for cc in range(2) for j in range(8) if UNITS[cc][j] == (d, source)) for source in range(2)]
         host, j = pick((hosts[0][0], hosts[1][0])), pick((hosts[0][1], hosts[1][1]))
-        for dy in (2, 1, 3):
-            peer = on_z(d, host)
-            peer["xc"] = peer["xc"] - y * 4 + lax.rem(y + dy, 4) * 4
-            send(blocks.at[lax.div(lax.rem(z + d, 8), 2)], mine, z_send, y_recv.at[1 if dy == 2 else 0, j], peer)
-    mine[...] = blocks[f]
+        block = blocks.at[SLOTS[d][0] + zl * (SLOTS[d][1] - SLOTS[d][0])]
+        peer = on_z(d, host)
+        send(block, mine, z_send, z_recv.at[j], peer)
+        for dy in DIRECT.get(d, ()):
+            on_y = {**peer, "xc": peer["xc"] - y * 4 + lax.rem(y + dy, 4) * 4}
+            send(block, mine, z_send, y_recv.at[1 if dy == 2 else 0, j], on_y)
+
+    for d in HALVES[0]:
+        hand_out(d)
+    gather(1, partial[1] + multiply(1, slice((CHUNKS - 1) * CHUNK, NFFT)))
+    for d in HALVES[1]:
+        hand_out(d)
+    mine[...] = blocks[3]
 
     def to_columns(j):
         for d in (1, 3, 2):
@@ -226,11 +245,12 @@
     def forward(j):
         block = place(0, j)
 
-        def to_rows():
-            for d, peer in y_peers.items():
-                send(block, block, y_send, y_recv.at[1 if d == 2 else 0, j], peer)
-
-        where(j, lambda dz: dz not in DIRECT, to_rows)
+        for d, peer in y_peers.items():
+            where(
+                j,
+                lambda dz: d not in DIRECT.get(dz, ()),
+                lambda: send(block, block, y_send, y_recv.at[1 if d == 2 else 0, j], peer),
+            )
 
     def share(dy, j):
         block = place(dy, j)
@@ -256,8 +276,8 @@
     for d in (0, 2, 6, 4):
         at = lax.div(lax.rem(z + 8 - d, 8), 2)
         cols[r, at] = rows[y, zl, core, at]
-    done_blocks((7 + 3 * len(DIRECT),) * 2, z_send)
-    done_blocks([3 * sum(dz not in DIRECT for dz, _ in units) for units in UNITS], y_send)
+    done_blocks((7 + sum(map(len, DIRECT.values())),) * 2, z_send)
+    done_blocks([sum(3 - len(DIRECT.get(dz, ())) for dz, _ in units) for units in UNITS], y_send)
     done_blocks([3 * sum(dz % 2 == 0 for dz, _ in units) for units in UNITS], x_send)
     done_blocks((32, 32), c_send)
 

time: 28.1 us -> 27.4 us (0.975)
  Pallas kernels: 28 us -> 27.3 us
    pallas_call x1, Pallas kernels: 24.1 us -> 23.4 us  [shards(): pl.pallas_call(spread, out_shape=[pltpu.VMEM((4, 2, 2, 4, 2, 16, 128), jn...]
where the time goes in v5:
time: 27.4 us; the launch traced here: 27.3 us
  Pallas kernels  27.3 us (100%)
    pallas_call x1, Pallas kernels, shards(): pl.pallas_call(spread, out_shape=[pltpu.VMEM((4, 2, 2, 4, 2, 16, 128), jn...  23.4 us
    pallas_call x1, Pallas kernels, shards(): pl.pallas_call(correlate, out_shape=jax.ShapeDtypeStruct((8, 2, 1024, 256...  3.92 us

profile of v5, /device:TPU:1, one launch (start us, length us, event | category | flops | bytes accessed | tf_op | source)
XLA Modules:
  0.0 27.3 jit_solution(6521405921550559457)
XLA Ops:
  0.0 23.4 %spread.1 = (f32[4,2,2,4,2,16,128]{6,5,4,3,2,1,0:T(8,128)S(1)}, f32[4,4,2,16,128]{4,3,2,1,0:T(8,128)S(1)}) custom-call(s32[16,77824]{1,0:T(8,128)} %samples.1, s32[32]{0:T(128)} %kept_hbm.1, s32[16]{0:T(128)} %flags_hbm.1), custom_call_target="tpu_custom_call" | custom-call | tf_op jit(solution)/shard_map/spread/pallas_call | solution.py:328
  23.4 3.9 %correlate.1 = bf16[8,2,1024,256]{3,2,1,0:T(8,128)(2,1)} custom-call(f32[4,2,2,4,2,16,128]{6,5,4,3,2,1,0:T(8,128)S(1)} %get-tuple-element.7.rows, f32[4,4,2,16,128]{4,3,2,1,0:T(8,128)S(1)} %get-tuple-element.8.cols), custom_call_target="tpu_custom_call" | custom-call | tf_op jit(solution)/shard_map/correlate/pallas_call | solution.py:357

commit v6 on v5

--- a/solution.py
+++ b/solution.py
@@ -284,40 +284,49 @@
 
 def correlate(rows, cols, out, left, right, stage, out_sem):
     lane = lax.broadcasted_iota(jnp.int32, (256, 128), 1)
-    long_lane = lax.broadcasted_iota(jnp.int32, (1024, 128), 1)
     real_lane = (lane & 1) == 0
 
-    def write(channel, part):
-        return pltpu.make_async_copy(stage.at[channel, part], out.at[channel, part], out_sem)
-
-    for c_hi in range(2):
-        x = rows[:, :, :, :, c_hi].reshape(1024, 128)
+    def prepare_columns(c_hi, p):
+        c = cols[:, :, c_hi].reshape(256, 128) * (1.0 / SPEC)
+        mine = (lane >> 6) == p
+        straight = jnp.where(mine, c, pltpu.roll(c, 64, 1))
+        swapped = jnp.where(real_lane, -pltpu.roll(straight, 127, 1), pltpu.roll(straight, 1, 1))
+        for part, value in enumerate((straight, swapped)):
+            value_high = value.astype(jnp.bfloat16).astype(jnp.float32)
+            first = jnp.where(lane < 64, value_high, value - value_high)
+            second = jnp.where(mine, value_high, 0.0)
+            for e in range(2):
+                mask = ((lane >> 1) & 1) == e
+                right[c_hi * 4 + p * 2 + e, part] = jnp.concatenate(
+                    [jnp.where(mask, first, 0.0), jnp.where(mask, second, 0.0)], axis=1
+                ).astype(jnp.bfloat16)
+
+    def prepare_rows(c_hi, line):
+        x = rows[line, :, :, :, c_hi].reshape(256, 128)
         turned = pltpu.roll(x, 64, 1)
         high = x.astype(jnp.bfloat16)
-        left[c_hi, 0] = jnp.where(long_lane < 64, x, turned).astype(jnp.bfloat16)
-        left[c_hi, 1] = jnp.where(long_lane < 64, turned, x).astype(jnp.bfloat16)
-        left[c_hi, 2] = (x - high.astype(jnp.float32)).astype(jnp.bfloat16)
-        c = cols[:, :, c_hi].reshape(256, 128) * (1.0 / SPEC)
-        c_turned = pltpu.roll(c, 64, 1)
-        for p in range(2):
-            mine = (lane >> 6) == p
-            operand = jnp.concatenate([left[c_hi, p], left[c_hi, 2]], axis=1)
-            straight = jnp.where(mine, c, c_turned)
-            swapped = jnp.where(real_lane, -pltpu.roll(straight, 127, 1), pltpu.roll(straight, 1, 1))
-            for part, value in enumerate((straight, swapped)):
-                value_high = value.astype(jnp.bfloat16).astype(jnp.float32)
-                first = jnp.where(lane < 64, value_high, value - value_high)
-                second = jnp.where(mine, value_high, 0.0)
-                for e in range(2):
-                    mask = ((lane >> 1) & 1) == e
-                    channel = c_hi * 4 + p * 2 + e
-                    right[channel, part] = jnp.concatenate(
-                        [jnp.where(mask, first, 0.0), jnp.where(mask, second, 0.0)], axis=1
-                    ).astype(jnp.bfloat16)
-                    stage[channel, part] = lax.dot_general(
-                        operand, right[channel, part], NT, preferred_element_type=jnp.float32
-                    ).astype(jnp.bfloat16)
-                    write(channel, part).start()
+        at = slice(line * 256, line * 256 + 256)
+        left[c_hi, 0, at] = jnp.where(lane < 64, x, turned).astype(jnp.bfloat16)
+        left[c_hi, 1, at] = jnp.where(lane < 64, turned, x).astype(jnp.bfloat16)
+        left[c_hi, 2, at] = (x - high.astype(jnp.float32)).astype(jnp.bfloat16)
+
+    def multiply(c_hi, p, at):
+        operand = jnp.concatenate([left[c_hi, p, at], left[c_hi, 2, at]], axis=1)
+        for e in range(2):
+            for part in range(2):
+                channel = c_hi * 4 + p * 2 + e
+                stage[channel, part, at] = lax.dot_general(
+                    operand, right[channel, part], NT, preferred_element_type=jnp.float32
+                ).astype(jnp.bfloat16)
+                pltpu.make_async_copy(stage.at[channel, part, at], out.at[channel, part, at], out_sem).start()
+
+    for c_hi in range(2):
+        prepare_columns(c_hi, 0)
+        for line in range(4):
+            prepare_rows(c_hi, line)
+            multiply(c_hi, 0, slice(line * 256, line * 256 + 256))
+        prepare_columns(c_hi, 1)
+        multiply(c_hi, 1, slice(0, 1024))
     pltpu.make_async_copy(stage, out, out_sem).wait()
 
 

time: 27.4 us -> 27.3 us (level)
  no operation moved by 1% of the time
where the time goes in v6:
time: 27.3 us; the launch traced here: 27.2 us
  Pallas kernels  27.2 us (100%)
    pallas_call x1, Pallas kernels, shards(): pl.pallas_call(spread, out_shape=[pltpu.VMEM((4, 2, 2, 4, 2, 16, 128), jn...  23.4 us
    pallas_call x1, Pallas kernels, shards(): pl.pallas_call(correlate, out_shape=jax.ShapeDtypeStruct((8, 2, 1024, 256...  3.8 us

profile of v6, /device:TPU:1, one launch (start us, length us, event | category | flops | bytes accessed | tf_op | source)
XLA Modules:
  0.0 27.2 jit_solution(4691878353036542378)
XLA Ops:
  0.0 23.4 %spread.1 = (f32[4,2,2,4,2,16,128]{6,5,4,3,2,1,0:T(8,128)S(1)}, f32[4,4,2,16,128]{4,3,2,1,0:T(8,128)S(1)}) custom-call(s32[16,77824]{1,0:T(8,128)} %samples.1, s32[32]{0:T(128)} %kept_hbm.1, s32[16]{0:T(128)} %flags_hbm.1), custom_call_target="tpu_custom_call" | custom-call | tf_op jit(solution)/shard_map/spread/pallas_call | solution.py:337
  23.4 3.8 %correlate.1 = bf16[8,2,1024,256]{3,2,1,0:T(8,128)(2,1)} custom-call(f32[4,2,2,4,2,16,128]{6,5,4,3,2,1,0:T(8,128)S(1)} %get-tuple-element.7.rows, f32[4,4,2,16,128]{4,3,2,1,0:T(8,128)S(1)} %get-tuple-element.8.cols), custom_call_target="tpu_custom_call" | custom-call | tf_op jit(solution)/shard_map/correlate/pallas_call | solution.py:366
